TPU v7x, 32 devices: a whole 2x2x4 slice. The times are simulated.
32 devices in a mesh: dom: 32 (over z, y, x, core).
Axes of the slice: x: 2, y: 2, z: 4, core: 2. Of those that a mesh axis runs over, the one named last changes fastest.
Arguments:
- element_freedom_values: float32 [9, 20, 32768], P(None, None, 'dom'), may hold values from -6 to 6
- scaled_jacobian_matrices: float32 [3, 9, 9, 32768], P(None, None, None, 'dom'), may hold values from -2 to 2
- outward_face_normals: float32 [4, 3, 32768], P(None, None, 'dom'), may hold values from -3 to 3
- largest_wave_speed: float32 [32768], P('dom'), may hold values from 0.5 to 2
- element_cluster_index: int32 [32768], P('dom'), may hold values 0 or 1
- element_new_slot: int32 [32768], P('dom'), may hold values from 0 to 36863, as said below
- neighbours: int32 [4, 32768], P(None, 'dom'), may hold values from 0 to 36607, as said below
- face_rotation_codes: int32 [4, 32768], P(None, 'dom'), may hold values from 0 to 11
- deriv_mats: float32 [3, 20, 20], replicated, may hold values from -1.25 to 1.25
- stiff_mats: float32 [3, 20, 20], replicated, may hold values from -1.25 to 1.25
- face_eval: float32 [12, 20, 16], replicated, may hold values from -1.25 to 1.25
- face_lift: float32 [4, 16, 20], replicated, may hold values from -1.5 to 1.5
Outputs:
- new_state: float32 [9, 20, 36864], P(None, None, 'dom')
Inputs may be any that keep to these rules, and one draw needn't show every extreme that they name: `element_new_slot`: one to one into slots partition * 1152 + local slot. Element 896 + j of partition d either stays at its local index or, on partitions that shed work, goes with g = j div 16 to partition (d + max(g * 4, 1)) mod 32, local slot 1024 + g * 16 + j mod 16; a partition sheds all 128 such elements or none; elements below 896 stay. Partitions 0 and 31 receive all 8 groups. `neighbours`: each names an occupied slot whose local index is below 896, on the element's own partition after migration or on one at s partitions' distance, s in -4..4 or s = 16, cyclically; at most one face of an element lies off its partition; from the elements of one partition after migration at most 32 faces name any one other partition, and partition 0 is named by exactly 32 faces from each of the nine partitions at those distances.
All inputs are finite; a program needn't handle non-finite values. No bound on the sum of `element_cluster_index` on one device may be relied on, other than what follows from the above.
Results may differ from a plain program's by a relative error of at most 0.0001.
Values sent between devices are 32-bit elements; how exact they have to be, the bound alone decides.
No kernel may reach another device: no remote copies, remote signals or barrier semaphores. Data moves between devices by JAX's collectives and lax.ppermute only.
A program may use at most 256 MiB of HBM per device.

v0:
```python
import math

import jax
import jax.numpy as jnp
from jax import lax
from jax.experimental import pallas as pl
from jax.experimental.pallas import tpu as pltpu
from jax.sharding import PartitionSpec as P

NV = 9
NB = 20
NBP = 24
NQ = 16
NORDER = 4
GROUPS = 8
CSZ = 16
KEEP = 896
PARTITION_SLOTS = 1152
REQ = 32
PARTNERS = 9
ASKS = 16
LANES = 128
WIDE = 256
ROWS = 216
JAC_END = ROWS + 4 * NV * NV
PACK = 192
MSG = 256
FAR = 384
RECORD = 640
SMALL = 24
MESSAGE1 = REQ + 8

step_fast = 0.25
exact = lax.Precision.HIGHEST
f32 = jnp.float32
bf16 = jnp.bfloat16
i32 = jnp.int32

SPEED, CLUSTER, LINK, ORIENT, OCCUPIED = 12, 13, 14, 18, 22

PARAMS = pltpu.CompilerParams(vmem_limit_bytes=60 << 20)


def coefficients(lower, upper):
    return [
        (upper ** (degree + 1) - lower ** (degree + 1)) / math.factorial(degree + 1)
        for degree in range(NORDER)
    ]


FIRST = coefficients(0.0, step_fast)
SECOND = coefficients(step_fast, 2.0 * step_fast)


def partner_offsets(devices):
    return [1, 2, 3, 4, -1, -2, -3, -4, devices // 2]


def packed_row(quantity, basis):
    group, member = quantity // 3, quantity % 3
    inside = 16 * member + basis if basis < 16 else 48 + 4 * member + (basis - 16)
    return 64 * group + inside


def pack_three(members):
    a, b, c = members
    tail = a[16:24] + pltpu.roll(b[16:24], 4, 0)
    return jnp.concatenate([a[:16], b[:16], c[:16], tail, c[16:24]], axis=0)


def split(values):
    high = values.astype(bf16)
    low = (values - high.astype(f32)).astype(bf16)
    return high, low


def stacked(high, low):
    return jnp.concatenate([high, low, high], axis=0)


def dot(a, b):
    return jnp.dot(a, b, preferred_element_type=f32)


def dot_last(a, b):
    return lax.dot_general(a, b, (((1,), (1,)), ((), ())), preferred_element_type=f32)


def iota(shape, axis):
    return lax.broadcasted_iota(i32, shape, axis)


def one_hot(condition):
    return jnp.where(condition, 1.0, 0.0).astype(bf16)


def make_weights(deriv, stiff, evals, lift, w_pred, w_own, w_lift, w_table, square):
    def turned(matrix, rows, columns):
        square[...] = jnp.zeros((LANES, LANES), f32)
        square[:rows, :columns] = matrix
        return square[...].T[:NBP]

    column = iota((LANES, PACK), 1) & 63
    member = jnp.where(column < 48, column >> 4, (column - 48) >> 2)
    basis = jnp.where(column < 48, column & 15, 16 + (column & 3))
    spread = one_hot(iota((LANES, PACK), 0) == jnp.where(member < 3, basis, -1))
    member = member[:NBP]
    part = iota((NBP, PACK), 1)

    def three(matrix):
        high, low = split(turned(matrix, NB, NB))
        row = jnp.where(part < 128, dot(high, spread), dot(low, spread))
        return [jnp.where(member == inner, row, 0.0) for inner in range(3)]

    blocks = []
    for axis in range(3):
        blocks += three(-deriv[axis])
    w_pred[...] = jnp.concatenate(blocks, axis=0).astype(bf16)

    own = [
        lax.dot_general(
            evals[48 * face : 48 * face + NQ, :],
            lift[face],
            (((0,), (0,)), ((), ())),
            precision=exact,
            preferred_element_type=f32,
        )
        for face in range(4)
    ]
    blocks = []
    for matrix in [stiff[axis] for axis in range(3)] + own + [own[0] + own[1] + own[2] + own[3]]:
        blocks += three(matrix if len(blocks) < 9 else -0.5 * matrix)
    w_own[...] = jnp.concatenate(blocks, axis=0).astype(bf16)

    column = iota((LANES, 144), 1)
    spread = one_hot(iota((LANES, 144), 0) == (column & 15))
    column = column[:NBP]
    block = column >> 4
    member = block - jnp.where(column >= 96, 6, jnp.where(column >= 48, 3, 0))
    for face in range(4):
        high, low = split(turned(lift[face], NQ, NB))
        row = jnp.where(column < 96, dot(high, spread), dot(low, spread))
        rows = [jnp.where(member == inner, -0.5 * row, 0.0) for inner in range(3)]
        w_lift[face] = jnp.concatenate(rows + [-r for r in rows], axis=0).astype(bf16)

    basis_of = one_hot((iota((320, NB), 0) >> 4) == iota((320, NB), 1))
    keep = (iota((320, PACK), 0) & 15) == (iota((320, PACK), 1) & 15)
    code_of = one_hot((iota((PACK, 16), 0) >> 4) == iota((PACK, 16), 1))
    halves = []
    for part_of in split(evals[...]):
        halves.append(dot(jnp.where(keep, dot_last(basis_of, part_of), 0.0).astype(bf16), code_of))
    w_table[:, :16] = halves[0].astype(bf16)
    w_table[:, 16:] = halves[1].astype(bf16)


def find_links(devices, tiles, small, aux, from_top):
    me = lax.axis_index("dom").astype(f32)
    row = iota((ASKS, LANES), 0).astype(f32)
    up_to = one_hot(iota((LANES, LANES), 0) <= iota((LANES, LANES), 1))
    request = (iota((LANES, LANES), 0) & (REQ - 1)).astype(f32)
    carry = jnp.zeros((ASKS, 1), f32)
    wanted = jnp.zeros((2 * ASKS, LANES), f32)
    for tile in range(tiles):
        at = slice(tile * LANES, (tile + 1) * LANES)
        occupied = small[OCCUPIED : OCCUPIED + 1, at] > 0.5
        target = jnp.full((1, LANES), -1.0, f32)
        slots = jnp.zeros((1, LANES), f32)
        for face in range(4):
            link = small[LINK + face : LINK + face + 1, at]
            owner = jnp.floor((link + 0.5) * (1.0 / PARTITION_SLOTS))
            slot = link - owner * PARTITION_SLOTS
            near = owner == me
            aux[face : face + 1, at] = jnp.where(near, slot, -1.0).astype(i32)
            away = occupied & jnp.logical_not(near)
            target = jnp.where(away, owner, target)
            slots = jnp.where(away, slot, slots)
        far = target - me
        far = jnp.where(far < 0, far + devices, far)
        partner = jnp.where(far <= 4, far - 1.0, jnp.where(far >= devices - 4, devices + 3.0 - far, 8.0))
        partner = jnp.where(target >= 0, partner, -1.0)
        named = jnp.where(row == partner, 1.0, 0.0)
        prefix = dot(named.astype(bf16), up_to) + carry
        carry = carry + jnp.sum(named, axis=1, keepdims=True)
        rank = jnp.sum(named * prefix, axis=0, keepdims=True) - 1.0
        if from_top:
            rank = REQ - 1.0 - rank
        aux[4:5, at] = jnp.where(target >= 0, partner * REQ + rank, -1.0).astype(i32)
        aux[5:8, at] = jnp.zeros((3, LANES), i32)
        ask = slots + 1.0
        high = jnp.floor(ask * (1.0 / 32)) * 32.0
        both = jnp.concatenate([named * high, named * (ask - high)], axis=0).astype(bf16)
        wanted = wanted + dot_last(both, one_hot(request == rank))
    return wanted[:ASKS] + wanted[ASKS:]


def prepare_kernel(devices, tiles, normals, speed, cluster, slot, links, orient, q, jac, small, aux, asks, group, one, record):
    me = lax.axis_index("dom")
    for face in range(4):
        small[3 * face : 3 * face + 3, :] = jnp.concatenate([normals[d, face : face + 1, :] for d in range(3)], axis=0)
    small[SPEED : SPEED + 1, :] = speed[...]
    small[CLUSTER : CLUSTER + 1, :] = cluster[...].astype(f32)
    small[LINK : LINK + 4, :] = links[...].astype(f32)
    small[ORIENT : ORIENT + 4, :] = orient[...].astype(f32)
    where = slot[...]
    stays = (where >= me * PARTITION_SLOTS) & (where < (me + 1) * PARTITION_SLOTS)
    small[OCCUPIED : OCCUPIED + 1, :] = jnp.where(stays, 1.0, 0.0)
    small[OCCUPIED + 1 : SMALL, :] = jnp.zeros((1, tiles * LANES), f32)
    wanted = find_links(devices, tiles, small, aux, False)
    asks[...] = jnp.zeros((devices, 1, LANES), f32)
    for k, offset in enumerate(partner_offsets(devices)):
        asks[lax.rem(me + offset + devices, devices)] = wanted[k : k + 1]

    record[...] = jnp.zeros((RECORD, LANES), f32)
    for p in range(NV):
        record[p * NBP : p * NBP + NB] = q[p]
        for inner in range(NV):
            at = ROWS + 4 * (p * NV + inner)
            record[at : at + 3] = jac[p, inner]
    fields = small[:, KEEP:]
    row = iota(fields.shape, 0)
    record[JAC_END : JAC_END + SMALL] = jnp.where(row == OCCUPIED, 1.0 - fields, fields)
    whole = record[...]
    turned = jnp.concatenate([whole[c : c + LANES].T for c in range(0, RECORD, LANES)], axis=1)
    one[...] = turned[:CSZ]
    position = me // (devices // GROUPS)
    for g in range(GROUPS):
        group[lax.rem(position + g, GROUPS)] = turned[g * CSZ : (g + 1) * CSZ]


def prepare(normals, speed, cluster, slot, links, orient, q, jac, devices):
    count = q.shape[2]

    def body(*refs):
        prepare_kernel(devices, count // LANES, *refs)

    last = KEEP // LANES
    return pl.pallas_call(
        body,
        grid=(1,),
        in_specs=[
            whole_spec(normals),
            whole_spec(speed),
            whole_spec(cluster),
            whole_spec(slot),
            whole_spec(links),
            whole_spec(orient),
            pl.BlockSpec((NV, NB, LANES), lambda i: (0, 0, last)),
            pl.BlockSpec((NV, NV, 3, LANES), lambda i: (0, 0, 0, last)),
        ],
        out_specs=[
            pl.BlockSpec((SMALL, count), lambda i: (0, 0)),
            pl.BlockSpec((8, count), lambda i: (0, 0)),
            pl.BlockSpec((devices, 1, LANES), lambda i: (0, 0, 0)),
            pl.BlockSpec((GROUPS, CSZ, RECORD), lambda i: (0, 0, 0)),
            pl.BlockSpec((CSZ, RECORD), lambda i: (0, 0)),
        ],
        out_shape=[
            jax.ShapeDtypeStruct((SMALL, count), f32),
            jax.ShapeDtypeStruct((8, count), i32),
            jax.ShapeDtypeStruct((devices, 1, LANES), f32),
            jax.ShapeDtypeStruct((GROUPS, CSZ, RECORD), f32),
            jax.ShapeDtypeStruct((CSZ, RECORD), f32),
        ],
        scratch_shapes=[pltpu.VMEM((RECORD, LANES), f32)],
        compiler_params=PARAMS,
        name="prepare",
    )(normals, speed, cluster, slot, links, orient, q, jac)


def unpack(devices, group, one, q, jac, small, aux):
    position = lax.axis_index("dom") // (devices // GROUPS)
    rows = [one[...]]
    for g in range(1, GROUPS):
        rows.append(group[lax.rem(position - g + GROUPS, GROUPS)])
    whole = jnp.concatenate(rows, axis=0)
    turned = jnp.concatenate([whole[:, c : c + LANES].T for c in range(0, RECORD, LANES)], axis=0)
    for p in range(NV):
        q[p] = turned[p * NBP : p * NBP + NB]
        for inner in range(NV):
            at = ROWS + 4 * (p * NV + inner)
            jac[p, inner] = turned[at : at + 3]
    small[...] = turned[JAC_END : JAC_END + SMALL]
    return find_links(devices, 1, small, aux, True)


OUT_BLOCKS = {1: (0, 0), 4: (0, 1), -2: (0, 2), -1: (1, 0), -4: (1, 1), 2: (1, 2), 3: (2, 0), -3: (3, 0)}
IN_BLOCKS = {-1: (0, 0), 1: (1, 0), -3: (2, 0), -4: (2, 1), -2: (2, 2), 3: (3, 0), 4: (3, 1), 2: (3, 2)}


def put(outs, rows, k, devices):
    if k == PARTNERS - 1:
        return outs[4], 0
    array, block = OUT_BLOCKS[-partner_offsets(devices)[k]]
    return outs[array], block * rows


def take(messages, k, devices):
    if k == PARTNERS - 1:
        return messages[4], 0
    array, block = IN_BLOCKS[partner_offsets(devices)[k]]
    rows = messages[4].shape[0]
    return messages[array], block * rows


def picked(requests, fields):
    lane = iota((1, LANES), 1)
    tiles = []
    for at in range(0, 12, 4):
        four = [requests[min(at + n, PARTNERS - 1)] for n in range(4)]
        tiles.append(
            jnp.where(lane < 32, four[0], jnp.where(lane < 64, four[1], jnp.where(lane < 96, four[2], four[3])))
        )
    slots = (iota((KEEP, FAR), 0) + 1).astype(f32)
    return dot(fields, one_hot(slots == jnp.concatenate(tiles, axis=1)))


def message_rows(both):
    value = both[:PACK] + both[PACK:]
    return jnp.concatenate([value, jnp.zeros((MSG - PACK, FAR), f32)], axis=0).T


def back(k):
    return k if k == PARTNERS - 1 else (k + 4) % 8


def requests_here(devices, asks):
    me = lax.axis_index("dom")
    peers = [lax.rem(me - o + devices, devices) for o in partner_offsets(devices)]
    return [asks[p] for p in peers]


def unpack_kernel(devices, group, one, asks, field, q, jac, small, aux, *outs):
    moved = unpack(devices, group, one, q, jac, small, aux)
    rows = message_rows(picked(requests_here(devices, asks), field[...]))
    for k in range(PARTNERS):
        out, at = put(outs, MESSAGE1, k, devices)
        out[at : at + REQ] = rows[k * REQ : (k + 1) * REQ]
        out[at + REQ : at + MESSAGE1, :LANES] = jnp.broadcast_to(moved[back(k) : back(k) + 1, :], (8, LANES))
        out[at + REQ : at + MESSAGE1, LANES:] = jnp.zeros((8, MSG - LANES), f32)


def answer_again(devices, asks, got, field, later, outs):
    moved = []
    for k in range(PARTNERS):
        message, at = take(got, back(k), devices)
        moved.append(message[at + REQ : at + REQ + 1, :LANES])
    every = [a + b for a, b in zip(requests_here(devices, asks), moved)]
    rows = message_rows(picked(every, later))
    rows_first = message_rows(picked(moved, field))
    for k in range(PARTNERS):
        out, at = put(outs, 2 * REQ, k, devices)
        out[at : at + REQ] = rows[k * REQ : (k + 1) * REQ]
        out[at + REQ : at + 2 * REQ] = rows_first[k * REQ : (k + 1) * REQ]


def relay_kernel(got_plus, got_minus, own_plus, own_minus, on_plus, on_minus):
    rows = own_plus.shape[0]
    block = [slice(b * rows, (b + 1) * rows) for b in range(3)]
    on_plus[block[0]] = own_plus[...]
    on_plus[block[1]] = got_plus[block[1]]
    on_plus[block[2]] = got_minus[block[2]]
    on_minus[block[0]] = own_minus[...]
    on_minus[block[1]] = got_minus[block[1]]
    on_minus[block[2]] = got_plus[block[2]]


def message_shapes(rows):
    return [jax.ShapeDtypeStruct((rows * blocks, MSG), f32) for blocks in (3, 3, 1, 1, 1)]


def far_table(devices, part, messages):
    rows = []
    for k in range(PARTNERS):
        message, at = take(messages, k, devices)
        rows.append(message[at + part * REQ : at + (part + 1) * REQ, :])
    rows.append(jnp.zeros((FAR - PARTNERS * REQ, MSG), f32))
    turned = jnp.concatenate(rows, axis=0).T[:PACK]
    return jnp.concatenate(split(turned), axis=0)


def lanes(tile):
    return slice(tile * LANES, (tile + 1) * LANES)


def jacobian_apply(jac, tile, parts):
    result = [None] * NV
    for group in range(3):
        for d in range(3):
            for inner in range(3):
                q = 3 * group + inner
                value = parts(d, q)
                for p in range(NV):
                    term = jac[p, q, d : d + 1, lanes(tile)] * value
                    result[p] = term if result[p] is None else result[p] + term
    return result


def packed_split(fields, group):
    packed = [pack_three(tile[3 * group : 3 * group + 3]) for tile in fields]
    return split(jnp.concatenate(packed, axis=1))


def split_fields(fields):
    pairs = [packed_split(fields, group) for group in range(3)]
    return jnp.concatenate([a for a, _ in pairs] + [b for _, b in pairs], axis=0)


def predict(start, jac, w_pred, scales):
    tiles = range(len(start))
    sums = [[[s[0] * x for x in tile] for tile in start] for s in scales]
    now = start
    for degree in range(1, NORDER):
        turned = [dot(w_pred, stacked(*packed_split(now, group))) for group in range(3)]
        now = [
            jacobian_apply(
                jac, t, lambda d, q: turned[q // 3][d * 72 + (q % 3) * NBP : d * 72 + (q % 3) * NBP + NBP, lanes(t)]
            )
            for t in tiles
        ]
        sums = [
            [[a + s[degree] * x for a, x in zip(total[t], now[t])] for t in tiles] for total, s in zip(sums, scales)
        ]
    return sums


def update(own, near, far, small, aux, jac, w_own, w_lift, w_table, gathered):
    count = own.shape[1]
    tiles = range(count // LANES)
    place = aux[4:5, :]
    both = dot(far, one_hot(iota((FAR, count), 0) == place))
    remote = both[:PACK] + both[PACK:]
    slots = iota((KEEP, count), 0)
    codes = iota((16, count), 0).astype(f32)

    def gather(face):
        index = aux[face : face + 1, :]
        both = dot(near[...], one_hot(slots == index))
        take_far = (index < 0) & (place >= 0)
        gathered[face, :, :count] = both[:PACK] + both[PACK:] + jnp.where(take_far, remote, 0.0)
        code = one_hot(codes == small[ORIENT + face : ORIENT + face + 1, :])
        return dot(w_table, jnp.concatenate([code, code], axis=0))

    table = gather(0)
    mine = []
    for group in range(3):
        rows = slice(64 * group, 64 * group + 64)
        lower = slice(PACK + 64 * group, PACK + 64 * group + 64)
        mine.append(dot(w_own, stacked(own[rows], own[lower])))

    def of_own(block, q, t):
        at = block * 72 + (q % 3) * NBP
        return mine[q // 3][at : at + NBP, lanes(t)]

    volume = [[[of_own(d, q, t) for q in range(NV)] for d in range(3)] for t in tiles]
    upwind = [[of_own(7, q, t) for q in range(NV)] for t in tiles]
    for face in range(4):
        now = table
        if face < 3:
            table = gather(face + 1)
        outers = []
        for t in tiles:
            outer = [None] * NV
            for b in range(NB):
                values = now[b * NQ : (b + 1) * NQ, lanes(t)]
                for p in range(NV):
                    at = packed_row(p, b)
                    term = gathered[face, at : at + 1, lanes(t)] * values
                    outer[p] = term if outer[p] is None else outer[p] + term
            outers.append(outer)
        for group in range(3):
            joined = [jnp.concatenate(outer[3 * group : 3 * group + 3], axis=0) for outer in outers]
            lifted = dot(w_lift[face], stacked(*split(jnp.concatenate(joined, axis=1))))
            for t in tiles:
                for inner in range(3):
                    q = 3 * group + inner
                    at = inner * NBP
                    mixed = lifted[at : at + NBP, lanes(t)] + of_own(3 + face, q, t)
                    upwind[t][q] = upwind[t][q] + lifted[72 + at : 72 + at + NBP, lanes(t)]
                    for d in range(3):
                        normal = small[3 * face + d : 3 * face + d + 1, lanes(t)]
                        volume[t][d][q] = volume[t][d][q] + normal * mixed
    result = []
    for t in tiles:
        change = jacobian_apply(jac, t, lambda d, q: volume[t][d][q])
        speed = small[SPEED : SPEED + 1, lanes(t)]
        result.append([c + speed * u for c, u in zip(change, upwind[t])])
    return result


def load_state(q, padded):
    padded[:, NB:NBP, :] = jnp.zeros((NV, NBP - NB, padded.shape[2]), f32)
    for p in range(NV):
        padded[p, :NB, :] = q[p]
    return load_field(padded)


def load_field(ref):
    return [[ref[p, :, lanes(t)] for p in range(NV)] for t in range(ref.shape[2] // LANES)]


def store_field(ref, field):
    for t, tile in enumerate(field):
        for p in range(NV):
            ref[p, :, lanes(t)] = tile[p]


def store_result(out, base, change, small):
    for t in range(len(base)):
        occupied = small[OCCUPIED : OCCUPIED + 1, lanes(t)] > 0.5
        for p in range(NV):
            out[p, :, lanes(t)] = jnp.where(occupied, base[t][p] + change[t][p], 0.0)[:NB]


def first_kernel(q, jac, deriv, stiff, evals, lift, packed, slow, w_pred, w_own, w_lift, w_table, padded, square):
    @pl.when(pl.program_id(0) == 0)
    def _():
        make_weights(deriv, stiff, evals, lift, w_pred, w_own, w_lift, w_table, square)

    first, later = predict(load_state(q, padded), jac, w_pred[...], [FIRST, SECOND])
    packed[...] = split_fields(first)
    store_field(slow, later)


def middle_step(start, jac, small, slow, own, near, far, aux, weights, gathered):
    w_pred, w_own, w_lift, w_table = weights
    change = update(own, near, far, small, aux, jac, w_own, w_lift, w_table, gathered)
    base, midway, second = [], [], []
    fast = [small[CLUSTER : CLUSTER + 1, lanes(t)] < 0.5 for t in range(len(start))]
    for t in range(len(start)):
        base.append([a + b for a, b in zip(start[t], change[t])])
        midway.append([jnp.where(fast[t], a, b) for a, b in zip(base[t], start[t])])
    (later,) = predict(midway, jac, w_pred, [FIRST])
    for t in range(len(start)):
        second.append([jnp.where(fast[t], a, b) for a, b in zip(later[t], slow[t])])
    return base, split_fields(second)


def middle_kernel(devices, steps, q, jac, small, slow, own, near, aux, asks, *refs):
    messages = refs[:5]
    w_pred, w_own, w_lift, w_table, base, packed, *outs, padded, gathered, far = refs[5:]
    step = pl.program_id(0)

    @pl.when(step == 0)
    def _():
        far[...] = far_table(devices, 0, messages)

    weights = (w_pred[...], w_own[...], w_lift, w_table[...])
    now, second = middle_step(
        load_state(q, padded), jac, small, load_field(slow), own[...], near, far[...], aux, weights, gathered
    )
    store_field(base, now)
    packed[:, pl.ds(pl.multiple_of(step * WIDE, WIDE), WIDE)] = second

    @pl.when(step == steps - 1)
    def _():
        answer_again(devices, asks, messages, near[...], packed[:, :KEEP], outs)


def last_kernel(
    devices, steps, base, jac, small, own, later, aux, q_moved, jac_moved, small_moved, aux_moved, near, *refs
):
    messages = refs[:5]
    w_pred, w_own, w_lift, w_table, out, padded, gathered, far = refs[5:]
    step = pl.program_id(0)

    @pl.when(step == 0)
    def _():
        far[...] = far_table(devices, 0, messages)

    @pl.when(step < steps)
    def _():
        change = update(
            own[...], later, far[...], small, aux, jac, w_own[...], w_lift, w_table[...], gathered
        )
        store_result(out, load_field(base), change, small)

    @pl.when(step == steps)
    def _():
        weights = (w_pred[...], w_own[...], w_lift, w_table[...])
        start = load_state(q_moved, padded)
        first, slow = predict(start, jac_moved, weights[0], [FIRST, SECOND])
        now, second = middle_step(
            start, jac_moved, small_moved, slow, split_fields(first), near, far_table(devices, 1, messages), aux_moved,
            weights, gathered,
        )
        change = update(second, later, far[...], small_moved, aux_moved, jac_moved, *weights[1:], gathered)
        store_result(out, now, change, small_moved)


def whole_spec(array):
    rank = array.ndim
    return pl.BlockSpec(array.shape, lambda i: (0,) * rank)


def lane_spec(*lead, last=None):
    rank = len(lead)
    if last is None:
        return pl.BlockSpec(lead + (WIDE,), lambda i: (0,) * rank + (i,))
    return pl.BlockSpec(lead + (WIDE,), lambda i: (0,) * rank + (jnp.minimum(i, last),))


Q_SPEC = lane_spec(NV, NB)
J_SPEC = lane_spec(NV, NV, 3)
S_SPEC = lane_spec(SMALL)
A_SPEC = lane_spec(8)
F_SPEC = lane_spec(NV, NBP)
X_SPEC = lane_spec(2 * PACK)
N_SPEC = pl.BlockSpec((2 * PACK, KEEP), lambda i: (0, 0))


def scratch_of(width):
    return pltpu.VMEM((NV, NBP, width), f32), pltpu.VMEM((4, PACK, width), f32)


def per_device(
    element_freedom_values,
    scaled_jacobian_matrices,
    outward_face_normals,
    largest_wave_speed,
    element_cluster_index,
    element_new_slot,
    neighbours,
    face_rotation_codes,
    deriv_mats,
    stiff_mats,
    face_eval,
    face_lift,
):
    count = element_freedom_values.shape[2]
    steps = count // WIDE
    devices = lax.axis_size("dom")
    q = element_freedom_values
    jac = jnp.transpose(scaled_jacobian_matrices, (1, 2, 0, 3))

    def shift(array, by):
        return lax.ppermute(array, "dom", [(i, (i + by) % devices) for i in range(devices)])

    def swap(array, groups):
        return lax.all_to_all(array, "dom", split_axis=0, concat_axis=0, axis_index_groups=groups, tiled=True)

    def exchange(plus, minus, own_plus, own_minus, half):
        got_plus, got_minus, half = shift(plus, 1), shift(minus, -1), shift(half, devices // 2)
        on_plus, on_minus = pl.pallas_call(
            relay_kernel,
            out_shape=[jax.ShapeDtypeStruct(plus.shape, f32)] * 2,
            compiler_params=pltpu.CompilerParams(vmem_limit_bytes=4 << 20),
            name="relay",
        )(got_plus, got_minus, own_plus, own_minus)
        return got_plus, got_minus, shift(on_plus, 3), shift(on_minus, -3), half

    def on_ring(body):
        def kernel(*refs):
            body(devices, *refs)

        return kernel

    small, aux, asks, group, one = prepare(
        jnp.transpose(outward_face_normals, (1, 0, 2)),
        largest_wave_speed[None],
        element_cluster_index[None],
        element_new_slot[None],
        neighbours,
        face_rotation_codes,
        q,
        jac,
        devices,
    )
    asks = swap(asks, None)
    asks, group, one = lax.optimization_barrier((asks, group, one))
    stride = devices // GROUPS
    group = swap(group, [[r + stride * j for j in range(GROUPS)] for r in range(stride)])
    one = shift(one, 1)
    padded, gathered = scratch_of(WIDE)
    packed_shape = jax.ShapeDtypeStruct((2 * PACK, count), bf16)
    field_shape = jax.ShapeDtypeStruct((NV, NBP, count), f32)
    far = pltpu.VMEM((2 * PACK, FAR), bf16)
    weight_shapes = [
        jax.ShapeDtypeStruct((ROWS, PACK), bf16),
        jax.ShapeDtypeStruct((576, PACK), bf16),
        jax.ShapeDtypeStruct((4, 144, 144), bf16),
        jax.ShapeDtypeStruct((320, 32), bf16),
    ]
    evals = jnp.transpose(face_eval, (0, 2, 1)).reshape(12 * NQ, NB)
    matrices = [deriv_mats, stiff_mats, evals, face_lift]
    first, slow, *weights = pl.pallas_call(
        first_kernel,
        grid=(steps,),
        in_specs=[Q_SPEC, J_SPEC] + [whole_spec(m) for m in matrices],
        out_specs=[X_SPEC, F_SPEC] + [whole_spec(w) for w in weight_shapes],
        out_shape=[packed_shape, field_shape] + weight_shapes,
        scratch_shapes=[padded, pltpu.VMEM((LANES, LANES), f32)],
        compiler_params=PARAMS,
        name="first",
    )(q, jac, *matrices)

    moved_shapes = [
        jax.ShapeDtypeStruct((NV, NB, LANES), f32),
        jax.ShapeDtypeStruct((NV, NV, 3, LANES), f32),
        jax.ShapeDtypeStruct((SMALL, LANES), f32),
        jax.ShapeDtypeStruct((8, LANES), i32),
    ]
    out_shape = moved_shapes + message_shapes(MESSAGE1)
    *moved, m0, m1, m2, m3, m4 = pl.pallas_call(
        on_ring(unpack_kernel),
        grid=(1,),
        in_specs=[whole_spec(a) for a in (group, one, asks)] + [N_SPEC],
        out_specs=[whole_spec(o) for o in out_shape],
        out_shape=out_shape,
        compiler_params=PARAMS,
        name="unpack",
    )(group, one, asks, first)
    messages = exchange(m0, m1, m2, m3, m4)

    def middle(*refs):
        middle_kernel(devices, steps, *refs)

    out_shape = [field_shape, packed_shape] + message_shapes(2 * REQ)
    base, second, *answers = pl.pallas_call(
        middle,
        grid=(steps,),
        in_specs=[Q_SPEC, J_SPEC, S_SPEC, F_SPEC, X_SPEC, N_SPEC, A_SPEC, whole_spec(asks)]
        + [whole_spec(a) for a in (*messages, *weights)],
        out_specs=[F_SPEC] + [whole_spec(o) for o in out_shape[1:]],
        out_shape=out_shape,
        scratch_shapes=[padded, gathered, far],
        compiler_params=PARAMS,
        name="middle",
    )(q, jac, small, slow, first, first, aux, asks, *messages, *weights)
    messages = exchange(*answers)

    def last(*refs):
        last_kernel(devices, steps, *refs)

    end = steps - 1
    return pl.pallas_call(
        last,
        grid=(steps + 1,),
        in_specs=[
            lane_spec(NV, NBP, last=end),
            lane_spec(NV, NV, 3, last=end),
            lane_spec(SMALL, last=end),
            lane_spec(2 * PACK, last=end),
            N_SPEC,
            lane_spec(8, last=end),
        ]
        + [whole_spec(a) for a in moved]
        + [N_SPEC]
        + [whole_spec(a) for a in (*messages, *weights)],
        out_specs=Q_SPEC,
        out_shape=jax.ShapeDtypeStruct((NV, NB, PARTITION_SLOTS), f32),
        scratch_shapes=[scratch_of(LANES)[0], gathered, far],
        compiler_params=PARAMS,
        name="last",
    )(base, jac, small, second, second, aux, *moved, first, *messages, *weights)


def solution(mesh):
    placed = (
        P(None, None, "dom"),
        P(None, None, None, "dom"),
        P(None, None, "dom"),
        P("dom"),
        P("dom"),
        P("dom"),
        P(None, "dom"),
        P(None, "dom"),
        P(),
        P(),
        P(),
        P(),
    )
    return jax.shard_map(
        per_device, mesh=mesh, in_specs=placed, out_specs=P(None, None, "dom"), check_vma=False
    )
```

profile of v0, /device:TPU:0, one launch (start us, length us, event | category | flops | bytes accessed | tf_op | source)
XLA Modules:
  0.0 122.5 jit_solution(4166159400627074408)
XLA Ops:
  0.0 2.5 %prepare.1 = (f32[24,1024]{1,0:T(8,128)}, s32[8,1024]{1,0:T(8,128)}, f32[32,1,128]{2,1,0:T(1,128)}, f32[8,16,640]{2,1,0:T(8,128)}, f32[16,640]{1,0:T(8,128)}) custom-call(f32[3,4,1024]{2,1,0:T(4,128)} %bitcast.13, f32[1,1024]{1,0:T(1,128)} %bitcast.14, s32[1,1024]{1,0:T(1,128)} %bitcast.15, s32[1,1024]{1,0:T(1,128)} %bitcast.16, s32[4,1024]{1,0:T(4,128)} %refs_4_.1, ...), custom_call_target="tpu_custom_call" | custom-call | tf_op jit(solution)/shard_map/prepare/pallas_call | solution.py:237
  2.5 14.5 %all_to_all.10.refs_2_.refs_7_ = f32[32,1,128]{2,1,0:T(1,128)} all-to-all(f32[32,1,128]{2,1,0:T(1,128)} %get-tuple-element.43), channel_id=1, replica_groups=mesh['dom'=32] {'dom'}, dimensions={0} | all-to-all | bytes 32768 | tf_op jit(solution)/shard_map/all_to_all | solution.py:639
  17.0 3.4 %all-to-all-start.1 = ((f32[8,16,640]{2,1,0:T(8,128)}), f32[8,16,640]{2,1,0:T(8,128)S(1)}, u32[]{:S(2)}, u32[]{:S(2)}) async-start(f32[8,16,640]{2,1,0:T(8,128)} %get-tuple-element.47), calls=%async_computation.1 | async-start | bytes 655360 | tf_op jit(solution)/shard_map/all_to_all | solution.py:639
  20.4 0.1 collective-permute-start
  20.5 11.1 %first.1 = (bf16[384,1024]{1,0:T(8,128)(2,1)}, f32[9,24,1024]{2,1,0:T(8,128)}, bf16[216,192]{1,0:T(8,128)(2,1)}, bf16[576,192]{1,0:T(8,128)(2,1)}, bf16[4,144,14...) custom-call(f32[9,20,1024]{2,1,0:T(8,128)} %refs_0_.1, f32[9,9,3,1024]{3,2,1,0:T(4,128)} %bitcast.9, f32[3,20,20]{2,1,0:T(8,128)} %deriv.1, ...), custom_call_target="tpu_custom_call" | custom-call | tf_op jit(solution)/shard_map/first/pallas_call | solution.py:685
  31.6 0.6 copy-done.15
  32.2 0.1 copy-done.8
  32.4 2.9 %unpack.1 = (f32[9,20,128]{2,1,0:T(8,128)}, f32[9,9,3,128]{3,2,1,0:T(4,128)}, f32[24,128]{1,0:T(8,128)}, s32[8,128]{1,0:T(8,128)}, f32[120,256]{1,0:T(8,128)}, /...) custom-call(f32[8,16,640]{2,1,0:T(8,128)} %copy-done.8, f32[16,640]{1,0:T(8,128)} %copy-done.15, ...), custom_call_target="tpu_custom_call" | custom-call | tf_op jit(solution)/shard_map/unpack/pallas_call | solution.py:703
  35.2 0.6 collective-permute-start.1
  35.8 4.7 %collective-permute-start.2 = (f32[120,256]{1,0:T(8,128)}, f32[120,256]{1,0:T(8,128)S(1)}, u32[]{:S(2)}, u32[]{:S(2)}) collective-permute-start(f32[120,256]{1,0:T(8,128)} %get-tuple-element.50), channel_id=1, source_target_pairs={{0,31},{1,0},{2,1},{3,2},{4,3},{5,4},{6,5},{7,6},{8,7},{9,8},{10,9... | collective-permute-start | bytes 368648 | tf_op jit(solution)/shard_map/ppermute | solution.py:636
  40.6 2.9 %collective-permute-done.1.got_plus.refs_8_ = f32[120,256]{1,0:T(8,128)S(1)} collective-permute-done((f32[120,256]{1,0:T(8,128)}, f32[120,256]{1,0:T(8,128)S(1)}, u32[]{:S(2)}, u32[]{:S(2)}) %collective-permute-start.1) | collective-permute-done | bytes 122912 | tf_op jit(solution)/shard_map/ppermute | solution.py:636
  43.5 0.8 copy-done.6
  44.3 0.8 copy-done.7
  45.1 0.3 collective-permute-start.3
  45.4 4.2 %collective-permute-start.4 = (f32[120,256]{1,0:T(8,128)S(1)}, f32[120,256]{1,0:T(8,128)S(1)}, u32[]{:S(2)}, u32[]{:S(2)}) collective-permute-start(f32[120,256]{1,0:T(8,128)S(1)} %get-tuple-element.54), channel_id=1, source_target_pairs={{0,29},{1,30},{2,31},{3,0},{4,1},{5,2},{6,3},{7,4},{8,5},{9,6},{10... | collective-permute-start | bytes 368648 | tf_op jit(solution)/shard_map/ppermute | solution.py:636
  49.6 5.6 %collective-permute-done.5.refs_12_ = f32[40,256]{1,0:T(8,128)S(1)} collective-permute-done((f32[40,256]{1,0:T(8,128)}, f32[40,256]{1,0:T(8,128)S(1)}, u32[]{:S(2)}, u32[]{:S(2)}) %collective-permute-start.5) | collective-permute-done | bytes 40992 | tf_op jit(solution)/shard_map/ppermute | solution.py:636
  55.2 0.6 copy-done.14
  55.7 0.1 copy-done.11
  55.8 0.1 copy-done.12
  55.8 23.8 %middle.1 = (f32[9,24,1024]{2,1,0:T(8,128)}, bf16[384,1024]{1,0:T(8,128)(2,1)}, f32[192,256]{1,0:T(8,128)}, f32[192,256]{1,0:T(8,128)}, f32[64,256]{1,0:T(8,128)}, /*index=5*/f32[64,256]{1,0:T(8,128)}, f32[64,256]{1,0:T(8,128)}) custom-call(f32[9,20,1024]{2,1,0:T(8,128)} %refs_0_.1, f32[9,9,3,1024]{3,2,1,0:T(4,128)} %bitcast.10, ...), custom_call_target="tpu_custom_call" | custom-call | tf_op jit(solution)/shard_map/middle/pallas_call | solution.py:718
  79.6 0.1 collective-permute-start.6
  79.7 5.3 %collective-permute-start.7 = (f32[192,256]{1,0:T(8,128)}, f32[192,256]{1,0:T(8,128)S(1)}, u32[]{:S(2)}, u32[]{:S(2)}) collective-permute-start(f32[192,256]{1,0:T(8,128)} %get-tuple-element.67), channel_id=1, source_target_pairs={{0,31},{1,0},{2,1},{3,2},{4,3},{5,4},{6,5},{7,6},{8,7},{9,8},{10,9... | collective-permute-start | bytes 589832 | tf_op jit(solution)/shard_map/ppermute | solution.py:636
  85.0 3.6 %collective-permute-done.6.got_plus.refs_11_ = f32[192,256]{1,0:T(8,128)S(1)} collective-permute-done((f32[192,256]{1,0:T(8,128)}, f32[192,256]{1,0:T(8,128)S(1)}, u32[]{:S(2)}, u32[]{:S(2)}) %collective-permute-start.6) | collective-permute-done | bytes 196640 | tf_op jit(solution)/shard_map/ppermute | solution.py:636
  88.6 0.9 copy-done.4
  89.5 0.8 copy-done.5
  90.4 0.1 collective-permute-start.8
  90.4 4.4 %collective-permute-start.9 = (f32[192,256]{1,0:T(8,128)S(1)}, f32[192,256]{1,0:T(8,128)S(1)}, u32[]{:S(2)}, u32[]{:S(2)}) collective-permute-start(f32[192,256]{1,0:T(8,128)S(1)} %get-tuple-element.71), channel_id=1, source_target_pairs={{0,29},{1,30},{2,31},{3,0},{4,1},{5,2},{6,3},{7,4},{8,5},{9,6},{10... | collective-permute-start | bytes 589832 | tf_op jit(solution)/shard_map/ppermute | solution.py:636
  94.8 6.1 %collective-permute-done.10.refs_15_ = f32[64,256]{1,0:T(8,128)S(1)} collective-permute-done((f32[64,256]{1,0:T(8,128)}, f32[64,256]{1,0:T(8,128)S(1)}, u32[]{:S(2)}, u32[]{:S(2)}) %collective-permute-start.10) | collective-permute-done | bytes 65568 | tf_op jit(solution)/shard_map/ppermute | solution.py:636
  101.0 0.6 copy-done.13
  101.5 0.1 copy-done.9
  101.6 0.1 copy-done.10
  101.7 20.8 %last.1 = f32[9,20,1152]{2,1,0:T(8,128)} custom-call(f32[9,24,1024]{2,1,0:T(8,128)} %get-tuple-element.60.refs_0_, f32[9,9,3,1024]{3,2,1,0:T(4,128)} %bitcast.11, f32[24,1024]{1,0:T(8,128)} %get-tuple-element.39.refs_2_, bf16[384,1024]{1,0:T(8,128)(2,1)} %get-tuple-element.61.refs_3_.refs_4_, bf16[384,1024]{1,0:T(8,128)(2,1)} %get-tuple-element.61.refs_3_.refs_4_, ...), custom_call_target="tpu_custom_call" | custom-call | tf_op jit(solution)/shard_map/last/pallas_call | solution.py:735
  (32 shorter events, 0.1 us)
Async XLA Ops:
  17.0 14.7 %all-to-all-start.1 = ((f32[8,16,640]{2,1,0:T(8,128)}), f32[8,16,640]{2,1,0:T(8,128)S(1)}, u32[]{:S(2)}, u32[]{:S(2)}) async-start(f32[8,16,640]{2,1,0:T(8,128)} %get-tuple-element.47), calls=%async_computation.1 | async-start | bytes 655360 | tf_op jit(solution)/shard_map/all_to_all | solution.py:639
  20.4 11.2 %collective-permute-start = (f32[16,640]{1,0:T(8,128)}, f32[16,640]{1,0:T(8,128)S(1)}, u32[]{:S(2)}, u32[]{:S(2)}) collective-permute-start(f32[16,640]{1,0:T(8,128)} %get-tuple-element.48), channel_id=1, source_target_pairs={{0,1},{1,2},{2,3},{3,4},{4,5},{5,6},{6,7},{7,8},{8,9},{9,10},{10,1... | collective-permute-start | bytes 122888 | tf_op jit(solution)/shard_map/ppermute | solution.py:636
  31.6 0.6 copy-start.15
  31.6 0.7 copy-start.8
  35.2 8.2 %collective-permute-start.1 = (f32[120,256]{1,0:T(8,128)}, f32[120,256]{1,0:T(8,128)S(1)}, u32[]{:S(2)}, u32[]{:S(2)}) collective-permute-start(f32[120,256]{1,0:T(8,128)} %get-tuple-element.49), channel_id=1, source_target_pairs={{0,1},{1,2},{2,3},{3,4},{4,5},{5,6},{6,7},{7,8},{8,9},{9,10},{10,1... | collective-permute-start | bytes 368648 | tf_op jit(solution)/shard_map/ppermute | solution.py:636
  35.8 7.6 %collective-permute-start.2 = (f32[120,256]{1,0:T(8,128)}, f32[120,256]{1,0:T(8,128)S(1)}, u32[]{:S(2)}, u32[]{:S(2)}) collective-permute-start(f32[120,256]{1,0:T(8,128)} %get-tuple-element.50), channel_id=1, source_target_pairs={{0,31},{1,0},{2,1},{3,2},{4,3},{5,4},{6,5},{7,6},{8,7},{9,8},{10,9... | collective-permute-start | bytes 368648 | tf_op jit(solution)/shard_map/ppermute | solution.py:636
  43.5 11.7 %copy-start.2 = (f32[120,256]{1,0:T(8,128)}, f32[120,256]{1,0:T(8,128)S(1)}, u32[]{:S(2)}) copy-start(f32[120,256]{1,0:T(8,128)S(1)} %collective-permute-done.1.got_plus.refs_8_) | copy-start | bytes 368644
  43.5 11.7 %copy-start.3 = (f32[120,256]{1,0:T(8,128)}, f32[120,256]{1,0:T(8,128)S(1)}, u32[]{:S(2)}) copy-start(f32[120,256]{1,0:T(8,128)S(1)} %collective-permute-done.2.got_minus.refs_9_) | copy-start | bytes 368644
  43.5 0.8 copy-start.6
  44.3 0.8 copy-start.7
  45.1 10.1 %collective-permute-start.3 = (f32[120,256]{1,0:T(8,128)S(1)}, f32[120,256]{1,0:T(8,128)S(1)}, u32[]{:S(2)}, u32[]{:S(2)}) collective-permute-start(f32[120,256]{1,0:T(8,128)S(1)} %get-tuple-element.53), channel_id=1, source_target_pairs={{0,3},{1,4},{2,5},{3,6},{4,7},{5,8},{6,9},{7,10},{8,11},{9,12},{10... | collective-permute-start | bytes 368648 | tf_op jit(solution)/shard_map/ppermute | solution.py:636
  45.4 9.8 %collective-permute-start.4 = (f32[120,256]{1,0:T(8,128)S(1)}, f32[120,256]{1,0:T(8,128)S(1)}, u32[]{:S(2)}, u32[]{:S(2)}) collective-permute-start(f32[120,256]{1,0:T(8,128)S(1)} %get-tuple-element.54), channel_id=1, source_target_pairs={{0,29},{1,30},{2,31},{3,0},{4,1},{5,2},{6,3},{7,4},{8,5},{9,6},{10... | collective-permute-start | bytes 368648 | tf_op jit(solution)/shard_map/ppermute | solution.py:636
  49.6 5.6 %collective-permute-start.5 = (f32[40,256]{1,0:T(8,128)}, f32[40,256]{1,0:T(8,128)S(1)}, u32[]{:S(2)}, u32[]{:S(2)}) collective-permute-start(f32[40,256]{1,0:T(8,128)} %get-tuple-element.55), channel_id=1, source_target_pairs={{0,16},{1,17},{2,18},{3,19},{4,20},{5,21},{6,22},{7,23},{8,24},{9,... | collective-permute-start | bytes 122888 | tf_op jit(solution)/shard_map/ppermute | solution.py:636
  55.1 0.6 copy-start.14
  55.1 0.7 copy-start.11
  55.1 0.7 copy-start.12
  79.6 9.0 %collective-permute-start.6 = (f32[192,256]{1,0:T(8,128)}, f32[192,256]{1,0:T(8,128)S(1)}, u32[]{:S(2)}, u32[]{:S(2)}) collective-permute-start(f32[192,256]{1,0:T(8,128)} %get-tuple-element.66), channel_id=1, source_target_pairs={{0,1},{1,2},{2,3},{3,4},{4,5},{5,6},{6,7},{7,8},{8,9},{9,10},{10,1... | collective-permute-start | bytes 589832 | tf_op jit(solution)/shard_map/ppermute | solution.py:636
  79.7 8.9 %collective-permute-start.7 = (f32[192,256]{1,0:T(8,128)}, f32[192,256]{1,0:T(8,128)S(1)}, u32[]{:S(2)}, u32[]{:S(2)}) collective-permute-start(f32[192,256]{1,0:T(8,128)} %get-tuple-element.67), channel_id=1, source_target_pairs={{0,31},{1,0},{2,1},{3,2},{4,3},{5,4},{6,5},{7,6},{8,7},{9,8},{10,9... | collective-permute-start | bytes 589832 | tf_op jit(solution)/shard_map/ppermute | solution.py:636
  88.6 12.4 %copy-start = (f32[192,256]{1,0:T(8,128)}, f32[192,256]{1,0:T(8,128)S(1)}, u32[]{:S(2)}) copy-start(f32[192,256]{1,0:T(8,128)S(1)} %collective-permute-done.6.got_plus.refs_11_) | copy-start | bytes 589828
  88.6 12.4 %copy-start.1 = (f32[192,256]{1,0:T(8,128)}, f32[192,256]{1,0:T(8,128)S(1)}, u32[]{:S(2)}) copy-start(f32[192,256]{1,0:T(8,128)S(1)} %collective-permute-done.7.got_minus.refs_12_) | copy-start | bytes 589828
  88.6 0.9 copy-start.4
  89.5 0.8 copy-start.5
  90.4 10.6 %collective-permute-start.8 = (f32[192,256]{1,0:T(8,128)S(1)}, f32[192,256]{1,0:T(8,128)S(1)}, u32[]{:S(2)}, u32[]{:S(2)}) collective-permute-start(f32[192,256]{1,0:T(8,128)S(1)} %get-tuple-element.70), channel_id=1, source_target_pairs={{0,3},{1,4},{2,5},{3,6},{4,7},{5,8},{6,9},{7,10},{8,11},{9,12},{10... | collective-permute-start | bytes 589832 | tf_op jit(solution)/shard_map/ppermute | solution.py:636
  90.4 10.5 %collective-permute-start.9 = (f32[192,256]{1,0:T(8,128)S(1)}, f32[192,256]{1,0:T(8,128)S(1)}, u32[]{:S(2)}, u32[]{:S(2)}) collective-permute-start(f32[192,256]{1,0:T(8,128)S(1)} %get-tuple-element.71), channel_id=1, source_target_pairs={{0,29},{1,30},{2,31},{3,0},{4,1},{5,2},{6,3},{7,4},{8,5},{9,6},{10... | collective-permute-start | bytes 589832 | tf_op jit(solution)/shard_map/ppermute | solution.py:636
  94.8 6.1 %collective-permute-start.10 = (f32[64,256]{1,0:T(8,128)}, f32[64,256]{1,0:T(8,128)S(1)}, u32[]{:S(2)}, u32[]{:S(2)}) collective-permute-start(f32[64,256]{1,0:T(8,128)} %get-tuple-element.72), channel_id=1, source_target_pairs={{0,16},{1,17},{2,18},{3,19},{4,20},{5,21},{6,22},{7,23},{8,24},{9,... | collective-permute-start | bytes 196616 | tf_op jit(solution)/shard_map/ppermute | solution.py:636
  100.9 0.6 copy-start.13
  100.9 0.7 copy-start.9
  100.9 0.7 copy-start.10
where the time goes:
time: 123 us
  Pallas kernels  61.1 us (50%)
  starting transfers between devices  23.2 us (19%)
  waiting for transfers between devices  18.1 us (15%)
  blocking collectives  14.5 us (12%)
  local copies, waits for them, and re-layouts  5.44 us (4%)
    pallas_call x1, Pallas kernels, per_device(): pl.pallas_call(middle, grid=(steps,), in_specs=[Q_SPEC, J_SPEC, S_SPEC, F...  23.8 us
    pallas_call x1, Pallas kernels, per_device(): pl.pallas_call(last, grid=(steps + 1,), in_specs=[lane_spec(NV, NBP, last...  20.8 us
    ppermute x11, starting transfers between devices, shift(): lax.ppermute(array, 'dom', [(i, (i + by) % devices) for i in range(device...  19.8 us
    ppermute x11, waiting for transfers between devices, shift(): lax.ppermute(array, 'dom', [(i, (i + by) % devices) for i in range(device...  18.1 us
    all_to_all x1, blocking collectives, swap(): lax.all_to_all(array, 'dom', split_axis=0, concat_axis=0, axis_index_grou...  14.5 us
    pallas_call x1, Pallas kernels, per_device(): pl.pallas_call(first_kernel, grid=(steps,), in_specs=[Q_SPEC, J_SPEC] + [...  11.1 us
    unnamed x32, local copies, waits for them, and re-layouts  5.44 us
    all_to_all x1, starting transfers between devices, swap(): lax.all_to_all(array, 'dom', split_axis=0, concat_axis=0, axis_index_grou...  3.43 us
  transfers between devices with their start and end apart: 12, of which 4 were waited for; matrix products, arithmetic and copies ran while one was open for 0% of the time, Pallas kernels for 9%

commit v1 on v0

--- a/solution.py
+++ b/solution.py
@@ -94,7 +94,7 @@
     return jnp.where(condition, 1.0, 0.0).astype(bf16)
 
 
-def make_weights(deriv, stiff, evals, lift, w_pred, w_own, w_lift, w_table, square):
+def make_weights(deriv, stiff, evals, lift, w_pred, w_own, w_lift, w_table, w_far, square):
     def turned(matrix, rows, columns):
         square[...] = jnp.zeros((LANES, LANES), f32)
         square[:rows, :columns] = matrix
@@ -137,11 +137,14 @@
     column = column[:NBP]
     block = column >> 4
     member = block - jnp.where(column >= 96, 6, jnp.where(column >= 48, 3, 0))
+    every = []
     for face in range(4):
         high, low = split(turned(lift[face], NQ, NB))
         row = jnp.where(column < 96, dot(high, spread), dot(low, spread))
         rows = [jnp.where(member == inner, -0.5 * row, 0.0) for inner in range(3)]
         w_lift[face] = jnp.concatenate(rows + [-r for r in rows], axis=0).astype(bf16)
+        every += rows
+    w_far[...] = jnp.concatenate(every, axis=0).astype(bf16)
 
     basis_of = one_hot((iota((320, NB), 0) >> 4) == iota((320, NB), 1))
     keep = (iota((320, PACK), 0) & 15) == (iota((320, PACK), 1) & 15)
@@ -423,22 +426,37 @@
     return sums
 
 
-def update(own, near, far, small, aux, jac, w_own, w_lift, w_table, gathered):
+def face_products(gathered, at_face, table, tiles):
+    outers = []
+    for t in tiles:
+        outer = [None] * NV
+        for b in range(NB):
+            values = table[b * NQ : (b + 1) * NQ, lanes(t)]
+            for p in range(NV):
+                at = packed_row(p, b)
+                term = gathered[at_face, at : at + 1, lanes(t)] * values
+                outer[p] = term if outer[p] is None else outer[p] + term
+        outers.append(outer)
+    return [
+        stacked(*split(jnp.concatenate([jnp.concatenate(o[3 * g : 3 * g + 3], axis=0) for o in outers], axis=1)))
+        for g in range(3)
+    ]
+
+
+def table_of(code, w_table):
+    hot = one_hot(iota((16, code.shape[1]), 0).astype(f32) == code)
+    return dot(w_table, jnp.concatenate([hot, hot], axis=0))
+
+
+def near_part(own, near, small, aux, w_own, w_lift, w_table, gathered):
     count = own.shape[1]
     tiles = range(count // LANES)
-    place = aux[4:5, :]
-    both = dot(far, one_hot(iota((FAR, count), 0) == place))
-    remote = both[:PACK] + both[PACK:]
     slots = iota((KEEP, count), 0)
-    codes = iota((16, count), 0).astype(f32)
 
     def gather(face):
-        index = aux[face : face + 1, :]
-        both = dot(near[...], one_hot(slots == index))
-        take_far = (index < 0) & (place >= 0)
-        gathered[face, :, :count] = both[:PACK] + both[PACK:] + jnp.where(take_far, remote, 0.0)
-        code = one_hot(codes == small[ORIENT + face : ORIENT + face + 1, :])
-        return dot(w_table, jnp.concatenate([code, code], axis=0))
+        both = dot(near[...], one_hot(slots == aux[face : face + 1, :]))
+        gathered[face, :, :count] = both[:PACK] + both[PACK:]
+        return table_of(small[ORIENT + face : ORIENT + face + 1, :], w_table)
 
     table = gather(0)
     mine = []
@@ -457,19 +475,8 @@
         now = table
         if face < 3:
             table = gather(face + 1)
-        outers = []
-        for t in tiles:
-            outer = [None] * NV
-            for b in range(NB):
-                values = now[b * NQ : (b + 1) * NQ, lanes(t)]
-                for p in range(NV):
-                    at = packed_row(p, b)
-                    term = gathered[face, at : at + 1, lanes(t)] * values
-                    outer[p] = term if outer[p] is None else outer[p] + term
-            outers.append(outer)
-        for group in range(3):
-            joined = [jnp.concatenate(outer[3 * group : 3 * group + 3], axis=0) for outer in outers]
-            lifted = dot(w_lift[face], stacked(*split(jnp.concatenate(joined, axis=1))))
+        for group, points in enumerate(face_products(gathered, face, now, tiles)):
+            lifted = dot(w_lift[face], points)
             for t in tiles:
                 for inner in range(3):
                     q = 3 * group + inner
@@ -479,12 +486,58 @@
                     for d in range(3):
                         normal = small[3 * face + d : 3 * face + d + 1, lanes(t)]
                         volume[t][d][q] = volume[t][d][q] + normal * mixed
-    result = []
+    return volume, upwind
+
+
+def update(parts, far, small, aux, jac, w_far, w_table, gathered):
+    volume, upwind = parts
+    tiles = range(len(volume))
+    count = len(volume) * LANES
+    place = aux[4:5, :]
+    both = dot(far, one_hot(iota((FAR, count), 0) == place))
+    gathered[0, :, :count] = both[:PACK] + both[PACK:]
+    masks = [jnp.where((aux[face : face + 1, :] < 0) & (place >= 0), 1.0, 0.0) for face in range(4)]
+    code = masks[0] * small[ORIENT : ORIENT + 1, :]
+    normals = [masks[0] * small[d : d + 1, :] for d in range(3)]
+    for face in range(1, 4):
+        code = code + masks[face] * small[ORIENT + face : ORIENT + face + 1, :]
+        normals = [n + masks[face] * small[3 * face + d : 3 * face + d + 1, :] for d, n in enumerate(normals)]
+    changes = [[None] * NV for t in tiles]
+    volume = [[list(v) for v in tile] for tile in volume]
+    upwind = [list(tile) for tile in upwind]
+    for group, points in enumerate(face_products(gathered, 0, table_of(code, w_table), tiles)):
+        lifted = dot(w_far, points)
+        for t in tiles:
+            for inner in range(3):
+                q = 3 * group + inner
+                mixed = None
+                for face in range(4):
+                    at = 72 * face + inner * NBP
+                    term = masks[face][:, lanes(t)] * lifted[at : at + NBP, lanes(t)]
+                    mixed = term if mixed is None else mixed + term
+                upwind[t][q] = upwind[t][q] - mixed
+                for d in range(3):
+                    volume[t][d][q] = volume[t][d][q] + normals[d][:, lanes(t)] * mixed
     for t in tiles:
         change = jacobian_apply(jac, t, lambda d, q: volume[t][d][q])
         speed = small[SPEED : SPEED + 1, lanes(t)]
-        result.append([c + speed * u for c, u in zip(change, upwind[t])])
-    return result
+        changes[t] = [c + speed * u for c, u in zip(change, upwind[t])]
+    return changes
+
+
+def store_parts(ref, parts):
+    volume, upwind = parts
+    for t in range(len(volume)):
+        for q in range(NV):
+            for d in range(3):
+                ref[d * NV + q, :, lanes(t)] = volume[t][d][q]
+            ref[3 * NV + q, :, lanes(t)] = upwind[t][q]
+
+
+def load_parts(ref):
+    tiles = range(ref.shape[2] // LANES)
+    volume = [[[ref[d * NV + q, :, lanes(t)] for q in range(NV)] for d in range(3)] for t in tiles]
+    return volume, [[ref[3 * NV + q, :, lanes(t)] for q in range(NV)] for t in tiles]
 
 
 def load_state(q, padded):
@@ -511,19 +564,23 @@
             out[p, :, lanes(t)] = jnp.where(occupied, base[t][p] + change[t][p], 0.0)[:NB]
 
 
-def first_kernel(q, jac, deriv, stiff, evals, lift, packed, slow, w_pred, w_own, w_lift, w_table, padded, square):
+def first_kernel(q, jac, deriv, stiff, evals, lift, packed, slow, w_pred, w_own, w_lift, w_table, w_far, padded, square):
     @pl.when(pl.program_id(0) == 0)
     def _():
-        make_weights(deriv, stiff, evals, lift, w_pred, w_own, w_lift, w_table, square)
+        make_weights(deriv, stiff, evals, lift, w_pred, w_own, w_lift, w_table, w_far, square)
 
     first, later = predict(load_state(q, padded), jac, w_pred[...], [FIRST, SECOND])
     packed[...] = split_fields(first)
     store_field(slow, later)
 
 
-def middle_step(start, jac, small, slow, own, near, far, aux, weights, gathered):
-    w_pred, w_own, w_lift, w_table = weights
-    change = update(own, near, far, small, aux, jac, w_own, w_lift, w_table, gathered)
+def near_kernel(own, near, small, aux, w_own, w_lift, w_table, *refs):
+    parts, gathered = refs[-2:]
+    store_parts(parts, near_part(own[...], near, small, aux, w_own[...], w_lift, w_table[...], gathered))
+
+
+def middle_step(start, parts, jac, small, slow, far, aux, w_pred, w_far, w_table, gathered):
+    change = update(parts, far, small, aux, jac, w_far, w_table, gathered)
     base, midway, second = [], [], []
     fast = [small[CLUSTER : CLUSTER + 1, lanes(t)] < 0.5 for t in range(len(start))]
     for t in range(len(start)):
@@ -535,18 +592,18 @@
     return base, split_fields(second)
 
 
-def middle_kernel(devices, steps, q, jac, small, slow, own, near, aux, asks, *refs):
+def middle_kernel(devices, steps, q, jac, small, slow, parts, near, aux, asks, *refs):
     messages = refs[:5]
-    w_pred, w_own, w_lift, w_table, base, packed, *outs, padded, gathered, far = refs[5:]
+    w_pred, w_far, w_table, base, packed, *outs, padded, gathered, far = refs[5:]
     step = pl.program_id(0)
 
     @pl.when(step == 0)
     def _():
         far[...] = far_table(devices, 0, messages)
 
-    weights = (w_pred[...], w_own[...], w_lift, w_table[...])
     now, second = middle_step(
-        load_state(q, padded), jac, small, load_field(slow), own[...], near, far[...], aux, weights, gathered
+        load_state(q, padded), load_parts(parts), jac, small, load_field(slow), far[...], aux,
+        w_pred[...], w_far[...], w_table[...], gathered,
     )
     store_field(base, now)
     packed[:, pl.ds(pl.multiple_of(step * WIDE, WIDE), WIDE)] = second
@@ -557,10 +614,10 @@
 
 
 def last_kernel(
-    devices, steps, base, jac, small, own, later, aux, q_moved, jac_moved, small_moved, aux_moved, near, *refs
+    devices, steps, base, jac, small, parts, aux, q_moved, jac_moved, small_moved, aux_moved, near, later, *refs
 ):
     messages = refs[:5]
-    w_pred, w_own, w_lift, w_table, out, padded, gathered, far = refs[5:]
+    w_pred, w_own, w_lift, w_table, w_far, out, padded, gathered, far = refs[5:]
     step = pl.program_id(0)
 
     @pl.when(step == 0)
@@ -569,21 +626,21 @@
 
     @pl.when(step < steps)
     def _():
-        change = update(
-            own[...], later, far[...], small, aux, jac, w_own[...], w_lift, w_table[...], gathered
-        )
+        change = update(load_parts(parts), far[...], small, aux, jac, w_far[...], w_table[...], gathered)
         store_result(out, load_field(base), change, small)
 
     @pl.when(step == steps)
     def _():
-        weights = (w_pred[...], w_own[...], w_lift, w_table[...])
         start = load_state(q_moved, padded)
-        first, slow = predict(start, jac_moved, weights[0], [FIRST, SECOND])
+        first, slow = predict(start, jac_moved, w_pred[...], [FIRST, SECOND])
+        of_near = w_own[...], w_lift, w_table[...]
+        own = near_part(split_fields(first), near, small_moved, aux_moved, *of_near, gathered)
         now, second = middle_step(
-            start, jac_moved, small_moved, slow, split_fields(first), near, far_table(devices, 1, messages), aux_moved,
-            weights, gathered,
+            start, own, jac_moved, small_moved, slow, far_table(devices, 1, messages), aux_moved,
+            w_pred[...], w_far[...], w_table[...], gathered,
         )
-        change = update(second, later, far[...], small_moved, aux_moved, jac_moved, *weights[1:], gathered)
+        own = near_part(second, later, small_moved, aux_moved, *of_near, gathered)
+        change = update(own, far[...], small_moved, aux_moved, jac_moved, w_far[...], w_table[...], gathered)
         store_result(out, now, change, small_moved)
 
 
@@ -637,16 +694,6 @@
 
     def swap(array, groups):
         return lax.all_to_all(array, "dom", split_axis=0, concat_axis=0, axis_index_groups=groups, tiled=True)
-
-    def exchange(plus, minus, own_plus, own_minus, half):
-        got_plus, got_minus, half = shift(plus, 1), shift(minus, -1), shift(half, devices // 2)
-        on_plus, on_minus = pl.pallas_call(
-            relay_kernel,
-            out_shape=[jax.ShapeDtypeStruct(plus.shape, f32)] * 2,
-            compiler_params=pltpu.CompilerParams(vmem_limit_bytes=4 << 20),
-            name="relay",
-        )(got_plus, got_minus, own_plus, own_minus)
-        return got_plus, got_minus, shift(on_plus, 3), shift(on_minus, -3), half
 
     def on_ring(body):
         def kernel(*refs):
@@ -679,10 +726,11 @@
         jax.ShapeDtypeStruct((576, PACK), bf16),
         jax.ShapeDtypeStruct((4, 144, 144), bf16),
         jax.ShapeDtypeStruct((320, 32), bf16),
+        jax.ShapeDtypeStruct((288, 144), bf16),
     ]
     evals = jnp.transpose(face_eval, (0, 2, 1)).reshape(12 * NQ, NB)
     matrices = [deriv_mats, stiff_mats, evals, face_lift]
-    first, slow, *weights = pl.pallas_call(
+    first, slow, w_pred, w_own, w_lift, w_table, w_far = pl.pallas_call(
         first_kernel,
         grid=(steps,),
         in_specs=[Q_SPEC, J_SPEC] + [whole_spec(m) for m in matrices],
@@ -709,29 +757,71 @@
         compiler_params=PARAMS,
         name="unpack",
     )(group, one, asks, first)
-    messages = exchange(m0, m1, m2, m3, m4)
+    of_near = [w_own, w_lift, w_table]
+    parts_shape = jax.ShapeDtypeStruct((4 * NV, NBP, count), f32)
+
+    def near_steps(field, begin, number, parts):
+        def spec(*lead):
+            rank = len(lead)
+            return pl.BlockSpec(lead + (WIDE,), lambda i: (0,) * rank + (i + begin,))
+
+        return pl.pallas_call(
+            near_kernel,
+            grid=(number,),
+            in_specs=[spec(2 * PACK), N_SPEC, spec(SMALL), spec(8)]
+            + [whole_spec(w) for w in of_near]
+            + [pl.BlockSpec(memory_space=pl.ANY)] * len(parts),
+            out_specs=spec(4 * NV, NBP),
+            out_shape=parts_shape,
+            scratch_shapes=[gathered],
+            input_output_aliases={7: 0} if parts else {},
+            cost_estimate=pl.CostEstimate(flops=int(2e9) * number, bytes_accessed=4 << 20, transcendentals=0),
+            compiler_params=PARAMS,
+            name="near",
+        )(field, field, small, aux, *of_near, *parts)
+
+    def exchange_beside(answers, field):
+        half = steps // 2
+        plus, minus, own_plus, own_minus, opposite = answers
+        got_plus, got_minus, opposite = shift(plus, 1), shift(minus, -1), shift(opposite, devices // 2)
+        parts = near_steps(field, 0, half, [])
+        got_plus, got_minus, opposite, parts = lax.optimization_barrier((got_plus, got_minus, opposite, parts))
+        on_plus, on_minus = pl.pallas_call(
+            relay_kernel,
+            out_shape=[jax.ShapeDtypeStruct(plus.shape, f32)] * 2,
+            compiler_params=pltpu.CompilerParams(vmem_limit_bytes=4 << 20),
+            name="relay",
+        )(got_plus, got_minus, own_plus, own_minus)
+        on_plus, on_minus = shift(on_plus, 3), shift(on_minus, -3)
+        parts = near_steps(field, half, steps - half, [parts])
+        return (got_plus, got_minus, on_plus, on_minus, opposite), parts
+
+    messages, parts = exchange_beside((m0, m1, m2, m3, m4), first)
 
     def middle(*refs):
         middle_kernel(devices, steps, *refs)
 
+    P_SPEC = lane_spec(4 * NV, NBP)
+    weights = [w_pred, w_far, w_table]
     out_shape = [field_shape, packed_shape] + message_shapes(2 * REQ)
     base, second, *answers = pl.pallas_call(
         middle,
         grid=(steps,),
-        in_specs=[Q_SPEC, J_SPEC, S_SPEC, F_SPEC, X_SPEC, N_SPEC, A_SPEC, whole_spec(asks)]
+        in_specs=[Q_SPEC, J_SPEC, S_SPEC, F_SPEC, P_SPEC, N_SPEC, A_SPEC, whole_spec(asks)]
         + [whole_spec(a) for a in (*messages, *weights)],
         out_specs=[F_SPEC] + [whole_spec(o) for o in out_shape[1:]],
         out_shape=out_shape,
         scratch_shapes=[padded, gathered, far],
         compiler_params=PARAMS,
         name="middle",
-    )(q, jac, small, slow, first, first, aux, asks, *messages, *weights)
-    messages = exchange(*answers)
+    )(q, jac, small, slow, parts, first, aux, asks, *messages, *weights)
+    messages, parts = exchange_beside(answers, second)
 
     def last(*refs):
         last_kernel(devices, steps, *refs)
 
     end = steps - 1
+    weights = [w_pred, w_own, w_lift, w_table, w_far]
     return pl.pallas_call(
         last,
         grid=(steps + 1,),
@@ -739,19 +829,18 @@
             lane_spec(NV, NBP, last=end),
             lane_spec(NV, NV, 3, last=end),
             lane_spec(SMALL, last=end),
-            lane_spec(2 * PACK, last=end),
-            N_SPEC,
+            lane_spec(4 * NV, NBP, last=end),
             lane_spec(8, last=end),
         ]
         + [whole_spec(a) for a in moved]
-        + [N_SPEC]
+        + [N_SPEC, N_SPEC]
         + [whole_spec(a) for a in (*messages, *weights)],
         out_specs=Q_SPEC,
         out_shape=jax.ShapeDtypeStruct((NV, NB, PARTITION_SLOTS), f32),
         scratch_shapes=[scratch_of(LANES)[0], gathered, far],
         compiler_params=PARAMS,
         name="last",
-    )(base, jac, small, second, second, aux, *moved, first, *messages, *weights)
+    )(base, jac, small, parts, aux, *moved, first, second, *messages, *weights)
 
 
 def solution(mesh):

time: 123 us -> 122 us (level)
  waiting for transfers between devices: 18.1 us -> 0.03 us
  Pallas kernels: 61.1 us -> 78.2 us
  local copies, waits for them, and re-layouts: 5.44 us -> 2.17 us
  starting transfers between devices: 23.2 us -> 26.1 us
    pallas_call x2 -> x6, Pallas kernels: 0.04 us -> 28.9 us  [the longest x4 28.9 us: near_steps(): pl.pallas_call(near_kernel, grid=(number,), in_specs=[spec(2 * PACK), N_S...]
    ppermute x11, waiting for transfers between devices: 18.1 us -> 0.03 us  [shift(): lax.ppermute(array, 'dom', [(i, (i + by) % devices) for i in range(device...]
    pallas_call x1, Pallas kernels: 23.8 us -> 17 us  [per_device(): pl.pallas_call(middle, grid=(steps,), in_specs=[Q_SPEC, J_SPEC, S_SPEC, F...]
    pallas_call x1, Pallas kernels: 20.8 us -> 15.8 us  [per_device(): pl.pallas_call(last, grid=(steps + 1,), in_specs=[lane_spec(NV, NBP, last...]
    unnamed x32, local copies, waits for them, and re-layouts: 5.44 us -> 2.17 us
    ppermute x11, starting transfers between devices: 19.8 us -> 22.6 us  [shift(): lax.ppermute(array, 'dom', [(i, (i + by) % devices) for i in range(device...]
  transfers between devices with their start and end apart: 12 -> 12, of which waited for: 4 -> 0; matrix products, arithmetic and copies ran while one was open for 0% -> 0% of each run, Pallas kernels for 9% -> 33%
where the time goes in v1:
time: 122 us; the launch traced here: 121 us
  Pallas kernels  78.2 us (64%)
  starting transfers between devices  26.1 us (21%)
  blocking collectives  14.3 us (12%)
  local copies, waits for them, and re-layouts  2.17 us (2%)
    pallas_call x4, Pallas kernels, near_steps(): pl.pallas_call(near_kernel, grid=(number,), in_specs=[spec(2 * PACK), N_S...  28.9 us
    ppermute x11, starting transfers between devices, shift(): lax.ppermute(array, 'dom', [(i, (i + by) % devices) for i in range(device...  22.6 us
    pallas_call x1, Pallas kernels, per_device(): pl.pallas_call(middle, grid=(steps,), in_specs=[Q_SPEC, J_SPEC, S_SPEC, F...  17 us
    pallas_call x1, Pallas kernels, per_device(): pl.pallas_call(last, grid=(steps + 1,), in_specs=[lane_spec(NV, NBP, last...  15.8 us
    all_to_all x1, blocking collectives, swap(): lax.all_to_all(array, 'dom', split_axis=0, concat_axis=0, axis_index_grou...  14.3 us
    pallas_call x1, Pallas kernels, per_device(): pl.pallas_call(first_kernel, grid=(steps,), in_specs=[Q_SPEC, J_SPEC] + [...  11.1 us
    all_to_all x1, starting transfers between devices, swap(): lax.all_to_all(array, 'dom', split_axis=0, concat_axis=0, axis_index_grou...  3.43 us
    pallas_call x1, Pallas kernels, per_device(): pl.pallas_call(on_ring(unpack_kernel), grid=(1,), in_specs=[whole_spec(a)...  2.87 us
  transfers between devices with their start and end apart: 12, of which 0 were waited for; matrix products, arithmetic and copies ran while one was open for 0% of the time, Pallas kernels for 33%

profile of v1, /device:TPU:0, one launch (start us, length us, event | category | flops | bytes accessed | tf_op | source)
XLA Modules:
  0.0 121.3 jit_solution(5638932365391101025)
XLA Ops:
  0.0 2.5 %prepare.1 = (f32[24,1024]{1,0:T(8,128)}, s32[8,1024]{1,0:T(8,128)}, f32[32,1,128]{2,1,0:T(1,128)}, f32[8,16,640]{2,1,0:T(8,128)}, f32[16,640]{1,0:T(8,128)}) custom-call(f32[3,4,1024]{2,1,0:T(4,128)} %bitcast.13, f32[1,1024]{1,0:T(1,128)} %bitcast.14, s32[1,1024]{1,0:T(1,128)} %bitcast.15, s32[1,1024]{1,0:T(1,128)} %bitcast.16, s32[4,1024]{1,0:T(4,128)} %refs_4_.1, ...), custom_call_target="tpu_custom_call" | custom-call | tf_op jit(solution)/shard_map/prepare/pallas_call | solution.py:240
  2.5 14.3 %all_to_all.10.refs_2_.refs_7_ = f32[32,1,128]{2,1,0:T(1,128)} all-to-all(f32[32,1,128]{2,1,0:T(1,128)} %get-tuple-element.55), channel_id=1, replica_groups=mesh['dom'=32] {'dom'}, dimensions={0} | all-to-all | bytes 32768 | tf_op jit(solution)/shard_map/all_to_all | solution.py:696
  16.8 3.4 %all-to-all-start.1 = ((f32[8,16,640]{2,1,0:T(8,128)}), f32[8,16,640]{2,1,0:T(8,128)S(1)}, u32[]{:S(2)}, u32[]{:S(2)}) async-start(f32[8,16,640]{2,1,0:T(8,128)} %get-tuple-element.58), calls=%async_computation.1 | async-start | bytes 655360 | tf_op jit(solution)/shard_map/all_to_all | solution.py:696
  20.3 0.1 collective-permute-start
  20.4 11.1 %first.1 = (bf16[384,1024]{1,0:T(8,128)(2,1)}, f32[9,24,1024]{2,1,0:T(8,128)}, bf16[216,192]{1,0:T(8,128)(2,1)}, bf16[576,192]{1,0:T(8,128)(2,1)}, bf16[4,144,14...) custom-call(f32[9,20,1024]{2,1,0:T(8,128)} %refs_0_.1, f32[9,9,3,1024]{3,2,1,0:T(4,128)} %bitcast.9, ...), custom_call_target="tpu_custom_call" | custom-call | tf_op jit(solution)/shard_map/first/pallas_call | solution.py:733
  31.5 0.0 collective-permute-done.refs_1_
  31.5 0.0 all-to-all-done.1.refs_0_
  31.5 0.6 copy-done.14
  32.1 0.1 copy-done.8
  32.3 2.9 %unpack.1 = (f32[9,20,128]{2,1,0:T(8,128)}, f32[9,9,3,128]{3,2,1,0:T(4,128)}, f32[24,128]{1,0:T(8,128)}, s32[8,128]{1,0:T(8,128)}, f32[120,256]{1,0:T(8,128)}, /...) custom-call(f32[8,16,640]{2,1,0:T(8,128)} %copy-done.8, f32[16,640]{1,0:T(8,128)} %copy-done.14, ...), custom_call_target="tpu_custom_call" | custom-call | tf_op jit(solution)/shard_map/unpack/pallas_call | solution.py:751
  35.1 2.7 %collective-permute-start.3 = (f32[40,256]{1,0:T(8,128)}, f32[40,256]{1,0:T(8,128)S(1)}, u32[]{:S(2)}, u32[]{:S(2)}) collective-permute-start(f32[40,256]{1,0:T(8,128)} %get-tuple-element.63), channel_id=1, source_target_pairs={{0,16},{1,17},{2,18},{3,19},{4,20},{5,21},{6,22},{7,23},{8,24},{9,... | collective-permute-start | bytes 122888 | tf_op jit(solution)/shard_map/ppermute | solution.py:693
  37.9 0.3 collective-permute-start.1
  38.2 5.0 %collective-permute-start.2 = (f32[120,256]{1,0:T(8,128)}, f32[120,256]{1,0:T(8,128)S(1)}, u32[]{:S(2)}, u32[]{:S(2)}) collective-permute-start(f32[120,256]{1,0:T(8,128)} %get-tuple-element.62), channel_id=1, source_target_pairs={{0,31},{1,0},{2,1},{3,2},{4,3},{5,4},{6,5},{7,6},{8,7},{9,8},{10,9... | collective-permute-start | bytes 368648 | tf_op jit(solution)/shard_map/ppermute | solution.py:693
  43.2 7.2 %near.4.refs_0_ = f32[36,24,1024]{2,1,0:T(8,128)} custom-call(bf16[384,1024]{1,0:T(8,128)(2,1)} %get-tuple-element.50.refs_3_.own.near.refs_5_.refs_9_, bf16[384,1024]{1,0:T(8,128)(2,1)} %get-tuple-element.50.refs_3_.own.near.refs_5_.refs_9_, f32[24,1024]{1,0:T(8,128)} %get-tuple-element.48.small.refs_2_, s32[8,1024]{1,0:T(8,128)} %get-tuple-element.51.aux.refs_6_.refs_4_, ...), custom_call_target="tpu_custom_call" | custom-call | flops 4000000000 | bytes 4194304 | tf_op jit(solution)/shard_map/near/pallas_call | solution.py:768
  50.5 0.0 collective-permute-done.3.refs_12_
  50.5 0.0 collective-permute-done.1.got_plus.refs_8_
  50.6 0.1 collective-permute-start.4
  50.6 4.4 %collective-permute-start.5 = (f32[120,256]{1,0:T(8,128)S(1)}, f32[120,256]{1,0:T(8,128)S(1)}, u32[]{:S(2)}, u32[]{:S(2)}) collective-permute-start(f32[120,256]{1,0:T(8,128)S(1)} %get-tuple-element.70), channel_id=1, source_target_pairs={{0,29},{1,30},{2,31},{3,0},{4,1},{5,2},{6,3},{7,4},{8,5},{9,6},{10... | collective-permute-start | bytes 368648 | tf_op jit(solution)/shard_map/ppermute | solution.py:693
  55.1 7.2 %near.5.refs_4_ = f32[36,24,1024]{2,1,0:T(8,128)} custom-call(bf16[384,1024]{1,0:T(8,128)(2,1)} %get-tuple-element.50.refs_3_.own.near.refs_5_.refs_9_, bf16[384,1024]{1,0:T(8,128)(2,1)} %get-tuple-element.50.refs_3_.own.near.refs_5_.refs_9_, f32[24,1024]{1,0:T(8,128)} %get-tuple-element.48.small.refs_2_, ...), custom_call_target="tpu_custom_call", output_to_operand_aliasing={{}: (7, {})} | custom-call | flops 4000000000 | bytes 4194304 | tf_op jit(solution)/shard_map/near/pallas_call | solution.py:768
  62.3 0.6 copy-done.11
  62.9 0.1 copy-done.12
  63.0 17.0 %middle.1 = (f32[9,24,1024]{2,1,0:T(8,128)}, bf16[384,1024]{1,0:T(8,128)(2,1)}, f32[192,256]{1,0:T(8,128)}, f32[192,256]{1,0:T(8,128)}, f32[64,256]{1,0:T(8,128)}, /*index=5*/f32[64,256]{1,0:T(8,128)}, f32[64,256]{1,0:T(8,128)}) custom-call(f32[9,20,1024]{2,1,0:T(8,128)} %refs_0_.1, f32[9,9,3,1024]{3,2,1,0:T(4,128)} %bitcast.10, ...), custom_call_target="tpu_custom_call" | custom-call | tf_op jit(solution)/shard_map/middle/pallas_call | solution.py:807
  80.0 0.1 collective-permute-start.8
  80.1 0.1 collective-permute-start.6
  80.2 5.3 %collective-permute-start.7 = (f32[192,256]{1,0:T(8,128)}, f32[192,256]{1,0:T(8,128)S(1)}, u32[]{:S(2)}, u32[]{:S(2)}) collective-permute-start(f32[192,256]{1,0:T(8,128)} %get-tuple-element.77), channel_id=1, source_target_pairs={{0,31},{1,0},{2,1},{3,2},{4,3},{5,4},{6,5},{7,6},{8,7},{9,8},{10,9... | collective-permute-start | bytes 589832 | tf_op jit(solution)/shard_map/ppermute | solution.py:693
  85.5 7.3 %near.6.refs_0_ = f32[36,24,1024]{2,1,0:T(8,128)} custom-call(bf16[384,1024]{1,0:T(8,128)(2,1)} %get-tuple-element.75.own.near.refs_10_, bf16[384,1024]{1,0:T(8,128)(2,1)} %get-tuple-element.75.own.near.refs_10_, f32[24,1024]{1,0:T(8,128)} %get-tuple-element.48.small.refs_2_, s32[8,1024]{1,0:T(8,128)} %get-tuple-element.51.aux.refs_6_.refs_4_, ...), custom_call_target="tpu_custom_call" | custom-call | flops 4000000000 | bytes 4194304 | tf_op jit(solution)/shard_map/near/pallas_call | solution.py:768
  92.9 0.1 collective-permute-start.9
  92.9 4.4 %collective-permute-start.10 = (f32[192,256]{1,0:T(8,128)S(1)}, f32[192,256]{1,0:T(8,128)S(1)}, u32[]{:S(2)}, u32[]{:S(2)}) collective-permute-start(f32[192,256]{1,0:T(8,128)S(1)} %get-tuple-element.89), channel_id=1, source_target_pairs={{0,29},{1,30},{2,31},{3,0},{4,1},{5,2},{6,3},{7,4},{8,5},{9,6},{10... | collective-permute-start | bytes 589832 | tf_op jit(solution)/shard_map/ppermute | solution.py:693
  97.4 7.2 %near.7.refs_3_ = f32[36,24,1024]{2,1,0:T(8,128)} custom-call(bf16[384,1024]{1,0:T(8,128)(2,1)} %get-tuple-element.75.own.near.refs_10_, bf16[384,1024]{1,0:T(8,128)(2,1)} %get-tuple-element.75.own.near.refs_10_, f32[24,1024]{1,0:T(8,128)} %get-tuple-element.48.small.refs_2_, ...), custom_call_target="tpu_custom_call", output_to_operand_aliasing={{}: (7, {})} | custom-call | flops 4000000000 | bytes 4194304 | tf_op jit(solution)/shard_map/near/pallas_call | solution.py:768
  104.6 0.6 copy-done.9
  105.3 0.1 copy-done.10
  105.3 15.8 %last.1 = f32[9,20,1152]{2,1,0:T(8,128)} custom-call(f32[9,24,1024]{2,1,0:T(8,128)} %get-tuple-element.74.refs_0_, f32[9,9,3,1024]{3,2,1,0:T(4,128)} %bitcast.11, f32[24,1024]{1,0:T(8,128)} %get-tuple-element.48.small.refs_2_, f32[36,24,1024]{2,1,0:T(8,128)} %near.7.refs_3_, s32[8,1024]{1,0:T(8,128)} %get-tuple-element.51.aux.refs_6_.refs_4_, ...), custom_call_target="tpu_custom_call" | custom-call | tf_op jit(solution)/shard_map/last/pallas_call | solution.py:825
  (36 shorter events, 0.1 us)
Async XLA Ops:
  16.8 14.7 %all-to-all-start.1 = ((f32[8,16,640]{2,1,0:T(8,128)}), f32[8,16,640]{2,1,0:T(8,128)S(1)}, u32[]{:S(2)}, u32[]{:S(2)}) async-start(f32[8,16,640]{2,1,0:T(8,128)} %get-tuple-element.58), calls=%async_computation.1 | async-start | bytes 655360 | tf_op jit(solution)/shard_map/all_to_all | solution.py:696
  20.3 11.2 %collective-permute-start = (f32[16,640]{1,0:T(8,128)}, f32[16,640]{1,0:T(8,128)S(1)}, u32[]{:S(2)}, u32[]{:S(2)}) collective-permute-start(f32[16,640]{1,0:T(8,128)} %get-tuple-element.59), channel_id=1, source_target_pairs={{0,1},{1,2},{2,3},{3,4},{4,5},{5,6},{6,7},{7,8},{8,9},{9,10},{10,1... | collective-permute-start | bytes 122888 | tf_op jit(solution)/shard_map/ppermute | solution.py:693
  31.5 0.6 copy-start.14
  31.5 0.7 copy-start.8
  35.1 15.3 %collective-permute-start.3 = (f32[40,256]{1,0:T(8,128)}, f32[40,256]{1,0:T(8,128)S(1)}, u32[]{:S(2)}, u32[]{:S(2)}) collective-permute-start(f32[40,256]{1,0:T(8,128)} %get-tuple-element.63), channel_id=1, source_target_pairs={{0,16},{1,17},{2,18},{3,19},{4,20},{5,21},{6,22},{7,23},{8,24},{9,... | collective-permute-start | bytes 122888 | tf_op jit(solution)/shard_map/ppermute | solution.py:693
  37.9 12.6 %collective-permute-start.1 = (f32[120,256]{1,0:T(8,128)}, f32[120,256]{1,0:T(8,128)S(1)}, u32[]{:S(2)}, u32[]{:S(2)}) collective-permute-start(f32[120,256]{1,0:T(8,128)} %get-tuple-element.61), channel_id=1, source_target_pairs={{0,1},{1,2},{2,3},{3,4},{4,5},{5,6},{6,7},{7,8},{8,9},{9,10},{10,1... | collective-permute-start | bytes 368648 | tf_op jit(solution)/shard_map/ppermute | solution.py:693
  38.2 12.3 %collective-permute-start.2 = (f32[120,256]{1,0:T(8,128)}, f32[120,256]{1,0:T(8,128)S(1)}, u32[]{:S(2)}, u32[]{:S(2)}) collective-permute-start(f32[120,256]{1,0:T(8,128)} %get-tuple-element.62), channel_id=1, source_target_pairs={{0,31},{1,0},{2,1},{3,2},{4,3},{5,4},{6,5},{7,6},{8,7},{9,8},{10,9... | collective-permute-start | bytes 368648 | tf_op jit(solution)/shard_map/ppermute | solution.py:693
  43.2 7.3 %copy-start.6 = (f32[40,256]{1,0:T(8,128)S(1)}, f32[40,256]{1,0:T(8,128)}, u32[]{:S(2)}) copy-start(f32[40,256]{1,0:T(8,128)} %get-tuple-element.67.own_plus) | copy-start | bytes 122884
  43.2 7.3 %copy-start.7 = (f32[40,256]{1,0:T(8,128)S(1)}, f32[40,256]{1,0:T(8,128)}, u32[]{:S(2)}) copy-start(f32[40,256]{1,0:T(8,128)} %get-tuple-element.68.own_minus) | copy-start | bytes 122884
  50.5 11.8 %copy-start.15 = (f32[40,256]{1,0:T(8,128)}, f32[40,256]{1,0:T(8,128)S(1)}, u32[]{:S(2)}) copy-start(f32[40,256]{1,0:T(8,128)S(1)} %collective-permute-done.3.refs_12_) | copy-start | bytes 122884
  50.5 11.8 %copy-start.2 = (f32[120,256]{1,0:T(8,128)}, f32[120,256]{1,0:T(8,128)S(1)}, u32[]{:S(2)}) copy-start(f32[120,256]{1,0:T(8,128)S(1)} %collective-permute-done.1.got_plus.refs_8_) | copy-start | bytes 368644
  50.5 11.8 %copy-start.3 = (f32[120,256]{1,0:T(8,128)}, f32[120,256]{1,0:T(8,128)S(1)}, u32[]{:S(2)}) copy-start(f32[120,256]{1,0:T(8,128)S(1)} %collective-permute-done.2.got_minus.refs_9_) | copy-start | bytes 368644
  50.6 11.7 %collective-permute-start.4 = (f32[120,256]{1,0:T(8,128)S(1)}, f32[120,256]{1,0:T(8,128)S(1)}, u32[]{:S(2)}, u32[]{:S(2)}) collective-permute-start(f32[120,256]{1,0:T(8,128)S(1)} %get-tuple-element.69), channel_id=1, source_target_pairs={{0,3},{1,4},{2,5},{3,6},{4,7},{5,8},{6,9},{7,10},{8,11},{9,12},{10... | collective-permute-start | bytes 368648 | tf_op jit(solution)/shard_map/ppermute | solution.py:693
  50.6 11.7 %collective-permute-start.5 = (f32[120,256]{1,0:T(8,128)S(1)}, f32[120,256]{1,0:T(8,128)S(1)}, u32[]{:S(2)}, u32[]{:S(2)}) collective-permute-start(f32[120,256]{1,0:T(8,128)S(1)} %get-tuple-element.70), channel_id=1, source_target_pairs={{0,29},{1,30},{2,31},{3,0},{4,1},{5,2},{6,3},{7,4},{8,5},{9,6},{10... | collective-permute-start | bytes 368648 | tf_op jit(solution)/shard_map/ppermute | solution.py:693
  62.3 0.7 copy-start.11
  62.3 0.7 copy-start.12
  80.0 12.7 %collective-permute-start.8 = (f32[64,256]{1,0:T(8,128)}, f32[64,256]{1,0:T(8,128)S(1)}, u32[]{:S(2)}, u32[]{:S(2)}) collective-permute-start(f32[64,256]{1,0:T(8,128)} %get-tuple-element.78), channel_id=1, source_target_pairs={{0,16},{1,17},{2,18},{3,19},{4,20},{5,21},{6,22},{7,23},{8,24},{9,... | collective-permute-start | bytes 196616 | tf_op jit(solution)/shard_map/ppermute | solution.py:693
  80.1 12.7 %collective-permute-start.6 = (f32[192,256]{1,0:T(8,128)}, f32[192,256]{1,0:T(8,128)S(1)}, u32[]{:S(2)}, u32[]{:S(2)}) collective-permute-start(f32[192,256]{1,0:T(8,128)} %get-tuple-element.76), channel_id=1, source_target_pairs={{0,1},{1,2},{2,3},{3,4},{4,5},{5,6},{6,7},{7,8},{8,9},{9,10},{10,1... | collective-permute-start | bytes 589832 | tf_op jit(solution)/shard_map/ppermute | solution.py:693
  80.2 12.6 %collective-permute-start.7 = (f32[192,256]{1,0:T(8,128)}, f32[192,256]{1,0:T(8,128)S(1)}, u32[]{:S(2)}, u32[]{:S(2)}) collective-permute-start(f32[192,256]{1,0:T(8,128)} %get-tuple-element.77), channel_id=1, source_target_pairs={{0,31},{1,0},{2,1},{3,2},{4,3},{5,4},{6,5},{7,6},{8,7},{9,8},{10,9... | collective-permute-start | bytes 589832 | tf_op jit(solution)/shard_map/ppermute | solution.py:693
  85.5 7.3 %copy-start.4 = (f32[64,256]{1,0:T(8,128)S(1)}, f32[64,256]{1,0:T(8,128)}, u32[]{:S(2)}) copy-start(f32[64,256]{1,0:T(8,128)} %get-tuple-element.86.own_plus) | copy-start | bytes 196612
  85.5 7.3 %copy-start.5 = (f32[64,256]{1,0:T(8,128)S(1)}, f32[64,256]{1,0:T(8,128)}, u32[]{:S(2)}) copy-start(f32[64,256]{1,0:T(8,128)} %get-tuple-element.87.own_minus) | copy-start | bytes 196612
  92.8 11.8 %copy-start.13 = (f32[64,256]{1,0:T(8,128)}, f32[64,256]{1,0:T(8,128)S(1)}, u32[]{:S(2)}) copy-start(f32[64,256]{1,0:T(8,128)S(1)} %collective-permute-done.8.refs_15_) | copy-start | bytes 196612
  92.8 11.8 %copy-start = (f32[192,256]{1,0:T(8,128)}, f32[192,256]{1,0:T(8,128)S(1)}, u32[]{:S(2)}) copy-start(f32[192,256]{1,0:T(8,128)S(1)} %collective-permute-done.6.got_plus.refs_11_) | copy-start | bytes 589828
  92.8 11.8 %copy-start.1 = (f32[192,256]{1,0:T(8,128)}, f32[192,256]{1,0:T(8,128)S(1)}, u32[]{:S(2)}) copy-start(f32[192,256]{1,0:T(8,128)S(1)} %collective-permute-done.7.got_minus.refs_12_) | copy-start | bytes 589828
  92.9 11.7 %collective-permute-start.9 = (f32[192,256]{1,0:T(8,128)S(1)}, f32[192,256]{1,0:T(8,128)S(1)}, u32[]{:S(2)}, u32[]{:S(2)}) collective-permute-start(f32[192,256]{1,0:T(8,128)S(1)} %get-tuple-element.88), channel_id=1, source_target_pairs={{0,3},{1,4},{2,5},{3,6},{4,7},{5,8},{6,9},{7,10},{8,11},{9,12},{10... | collective-permute-start | bytes 589832 | tf_op jit(solution)/shard_map/ppermute | solution.py:693
  92.9 11.7 %collective-permute-start.10 = (f32[192,256]{1,0:T(8,128)S(1)}, f32[192,256]{1,0:T(8,128)S(1)}, u32[]{:S(2)}, u32[]{:S(2)}) collective-permute-start(f32[192,256]{1,0:T(8,128)S(1)} %get-tuple-element.89), channel_id=1, source_target_pairs={{0,29},{1,30},{2,31},{3,0},{4,1},{5,2},{6,3},{7,4},{8,5},{9,6},{10... | collective-permute-start | bytes 589832 | tf_op jit(solution)/shard_map/ppermute | solution.py:693
  104.6 0.7 copy-start.9
  104.6 0.7 copy-start.10
